TPU v7x, 512 devices: a whole 4x4x16 slice. The times are simulated.
512 devices in a mesh: shift: 4 (over x), cells: 128 (over z, y, core).
Axes of the slice: x: 4, y: 4, z: 16, core: 2. Of those that a mesh axis runs over, the one named last changes fastest.
Arguments:
- perm: float32 [1024, 64, 256], P(('shift', 'cells')), parts along dimension 0, may hold values from 0.1 to 10
- storage: float32 [1024, 64, 256], P(('shift', 'cells')), parts along dimension 0, may hold values from 0.005 to 0.05
- right_side: float32 [1024, 64, 256], P(('shift', 'cells')), parts along dimension 0, may hold values from -15 to 15
- coupling: bfloat16 [16384, 64, 256], P('cells'), may hold values from -0.75 to 0.75
- gains: bfloat16 [16384, 64], P('cells'), may hold values from 0.5 to 2
- well_target: int32 [16384, 1], P('cells'), may hold values from 0 to 127; in each aligned block of 128 rows (0 to 127, 128 to 255, ...) at most 2 rows name the same one
- well_column: int32 [16384], P('cells'), may hold values from 0 to 127
Outputs:
- solution: float32 [1024, 64, 256], P(('shift', 'cells')), parts along dimension 0
- residual: float32 [1024, 64, 256], P(('shift', 'cells')), parts along dimension 0
There are 4 independent parts, one for each index of `shift`. A program takes and returns all parts, laid end to end along the dimension named above; an argument that names none is the same for every part. Nothing has to cross between parts.
Inputs may be any that keep to these rules, and one draw needn't show every extreme that they name: `well_target`: among the completions listed on one device, at most 2 name the same cell block, and some device has 2 naming one block.
All inputs are finite; a program needn't handle non-finite values.
Results may differ from a plain program's by a relative error of at most 0.0045.
Values may be sent and summed in bfloat16 or wider, within the bound.
A program may use at most 128 MiB of HBM per device.

v0:
```python
import jax
import jax.numpy as jnp
from jax import lax
from jax.sharding import PartitionSpec as P

ITERS = 2


def extended(cells, sides, width):
    for axis, dim in sides:
        count = lax.axis_size(axis)
        ends = count - 1
        head = lax.slice_in_dim(cells, 0, width, axis=dim)
        tail = lax.slice_in_dim(cells, cells.shape[dim] - width, cells.shape[dim], axis=dim)
        cells = jnp.concatenate(
            [
                lax.ppermute(tail, axis, [(i, (i + 1) % count) for i in range(ends)]),
                cells,
                lax.ppermute(head, axis, [((i + 1) % count, i) for i in range(ends)]),
            ],
            axis=dim,
        )
    return cells


def harmonic(first, second):
    return 2.0 * first * second / (first + second)


def precondition(values, trans_z, diagonal):
    lower = -trans_z[:, :, :-1]
    upper = -trans_z[:, :, 1:]
    return lax.linalg.tridiagonal_solve(lower, diagonal, upper, values[..., None])[..., 0]


def norm_sum(residual, smoothed):
    return lax.psum(jnp.sum(residual * smoothed), "cells")


def on_device(perm, storage, right_side, coupling, gains, well_target, well_column):
    devices = lax.axis_size("cells")
    comp_local = coupling.shape[0]
    perforations = coupling.shape[1]
    capacity = max(2, 2 * comp_local // devices)
    total_slots = devices * capacity
    width_x, width_y, width_z = perm.shape
    columns = width_x * width_y
    padded_perm = extended(perm, (("cells", 0),), 1)
    trans_x = harmonic(padded_perm[:-1], padded_perm[1:])
    pad_y = jnp.pad(perm, ((0, 0), (1, 1), (0, 0)))
    pad_z = jnp.pad(perm, ((0, 0), (0, 0), (1, 1)))
    trans_y = harmonic(pad_y[:, :-1], pad_y[:, 1:])
    trans_z = harmonic(pad_z[:, :, :-1], pad_z[:, :, 1:])
    diagonal = (
        storage
        + trans_x[:-1]
        + trans_x[1:]
        + trans_y[:, :-1]
        + trans_y[:, 1:]
        + trans_z[:, :, :-1]
        + trans_z[:, :, 1:]
    )
    target = well_target[:, 0]
    order = jnp.arange(comp_local, dtype=jnp.int32)
    earlier = (target[:, None] == target[None, :]) & (order[None, :] < order[:, None])
    slot_rank = jnp.sum(earlier.astype(jnp.int32), axis=1)
    destination = target * capacity + slot_rank
    send_cols = jnp.zeros((total_slots,), jnp.int32).at[destination].set(well_column)
    send_blocks = (
        jnp.zeros((total_slots, perforations, width_z), jnp.bfloat16).at[destination].set(coupling)
    )
    send_gains = jnp.zeros((total_slots, perforations), jnp.bfloat16).at[destination].set(gains)
    slot_blocks, slot_gains, slot_cols = (
        lax.all_to_all(send_blocks, "cells", split_axis=0, concat_axis=0, tiled=True),
        lax.all_to_all(send_gains, "cells", split_axis=0, concat_axis=0, tiled=True),
        lax.all_to_all(send_cols, "cells", split_axis=0, concat_axis=0, tiled=True),
    )
    solution = jnp.zeros_like(right_side)
    residual = right_side
    smoothed = precondition(residual, trans_z, diagonal)
    direction = smoothed
    norm_now = norm_sum(residual, smoothed)
    for iteration in range(ITERS):
        pad_x = extended(direction, (("cells", 0),), 1)
        field_y = jnp.pad(direction, ((0, 0), (1, 1), (0, 0)))
        field_z = jnp.pad(direction, ((0, 0), (0, 0), (1, 1)))
        result = diagonal * direction - trans_x[:-1] * pad_x[:-2] - trans_x[1:] * pad_x[2:]
        result = result - trans_y[:, :-1] * field_y[:, :-2] - trans_y[:, 1:] * field_y[:, 2:]
        result = (
            result - trans_z[:, :, :-1] * field_z[:, :, :-2] - trans_z[:, :, 1:] * field_z[:, :, 2:]
        )
        field_cols = direction.reshape(columns, width_z)
        rows = field_cols[slot_cols].astype(jnp.bfloat16)
        proj = jnp.einsum("kpc,kc->kp", slot_blocks, rows, preferred_element_type=jnp.float32)
        scaled = (proj * slot_gains.astype(jnp.float32)).astype(jnp.bfloat16)
        back = jnp.einsum("kpc,kp->kc", slot_blocks, scaled, preferred_element_type=jnp.float32)
        total = jnp.zeros((columns, width_z), jnp.float32).at[slot_cols].add(back)
        image = result + total.reshape(width_x, width_y, width_z)
        alpha = norm_now / lax.psum(jnp.sum(direction * image), "cells")
        solution = solution + alpha * direction
        residual = residual - alpha * image
        if iteration + 1 < ITERS:
            smoothed = precondition(residual, trans_z, diagonal)
            fresh = norm_sum(residual, smoothed)
            direction = smoothed + fresh / norm_now * direction
            norm_now = fresh
    return (solution, residual)


def solution(mesh):
    in_specs = (
        P(("shift", "cells"), None, None),
        P(("shift", "cells"), None, None),
        P(("shift", "cells"), None, None),
        P("cells", None, None),
        P("cells", None),
        P("cells", None),
        P("cells"),
    )
    out_specs = (P(("shift", "cells"), None, None), P(("shift", "cells"), None, None))
    return jax.shard_map(
        on_device, mesh=mesh, in_specs=in_specs, out_specs=out_specs, check_vma=False
    )
```

profile of v0, /device:TPU:1, one launch (start us, length us, event | category | flops | bytes accessed | tf_op | source)
XLA Modules:
  0.0 1452.9 jit_solution(9327977267852211826)
XLA Ops:
  0.6 0.9 fusion.1315
  1.5 4.6 collective-permute-start
  6.1 5.5 collective-permute-start.1
  11.6 0.9 convert_reduce_fusion
  13.2 1.1 scatter_custom_fusion
  15.1 16.7 %all-to-all-start = ((s32[128,2,1]{1,2,0:T(1,128)}), s32[128,2,1]{1,2,0:T(1,128)S(1)}, u32[]{:S(2)}, u32[]{:S(2)}) async-start(s32[128,2,1]{1,2,0:T(1,128)} %bitcast.981), calls=%async_computation | async-start | bytes 131072 | tf_op jit(solution)/shard_map/all_to_all | solution.py:76
  31.8 1.1 add_divide_fusion.1
  32.9 1.0 slice_bitcast_fusion.1
  35.3 1.0 add_divide_fusion.2
  36.3 0.8 copy.1080
  37.1 0.8 copy.1183
  37.9 1.5 scatter_custom_fusion.2
  39.4 4.3 broadcast_in_dim.2081
  43.7 19.3 %scatter_fusion = bf16[256,64,256]{2,1,0:T(8,128)(2,1)} fusion(bf16[256,64,256]{2,1,0:T(8,128)(2,1)} %broadcast_in_dim.2081, s32[128]{0:T(128)S(1)} %fusion.915, bf16[128,64,256]{2,1,0:T(8,128)(2,1)} %param.18), kind=kCustom, calls=%fused_computation.3 | custom fusion | bytes 12583424 | tf_op jit(solution)/shard_map/scatter | solution.py:70
  63.0 16.7 %all-to-all-start.1 = ((bf16[256,64,256]{2,1,0:T(8,128)(2,1)}), bf16[256,64,256]{2,1,0:T(8,128)(2,1)}, u32[]{:S(2)}, u32[]{:S(2)}) async-start(bf16[256,64,256]{2,1,0:T(8,128)(2,1)} %scatter_fusion), calls=%async_computation.1 | async-start | bytes 16777216 | tf_op jit(solution)/shard_map/all_to_all | solution.py:74
  80.3 0.8 reduce.344
  83.0 1.1 slice_reduce_fusion.32
  84.3 1.1 slice_reduce_fusion.69
  85.4 1.4 slice_reduce_fusion.31
  86.7 1.1 slice_reduce_fusion.152
  88.7 0.9 copy.1082
  89.7 0.9 copy.1083
  90.7 0.9 copy.1084
  91.7 173.9 %while.64 = (s32[]{:T(128)}, f32[2,64]{1,0:T(2,128)S(1)}, f32[2,64,1]{1,0,2:T(2,128)S(1)}, f32[7,32,2,64]{3,2,1,0:T(2,128)S(1)}, f32[7,32,2,64,1]{3,2,1,4,0:T(2,...) while((s32[]{:T(128)}, f32[2,64]{1,0:T(2,128)S(1)}, ...), condition=%wide.region_1.2_spmd, body=%wide.region_0.1_spmd.sunk | while | flops 32801 | bytes 458345 | solution.py:33
  286.5 4.3 while.65
  294.9 0.9 concatenate.94
  295.9 3.0 collective-permute-start.3
  298.9 2.5 collective-permute-start.2
  301.6 1.1 gather_fusion
  302.8 141.8 %all-to-all-done.1 = bf16[256,64,256]{2,1,0:T(8,128)(2,1)} async-done(((bf16[256,64,256]{2,1,0:T(8,128)(2,1)}), bf16[256,64,256]{2,1,0:T(8,128)(2,1)}, u32[]{:S(2)}, u32[]{:S(2)}) %all-to-all-start.1) | async-done | bytes 8388640 | tf_op jit(solution)/shard_map/all_to_all | solution.py:74
  444.6 11.5 all-to-all-start.2
  456.2 5.6 fusion.648
  461.8 9.2 all-to-all-done.2
  471.0 4.6 fusion.682
  476.0 2.1 scatter_custom_fusion.3
  478.1 0.8 multiply_reduce_fusion.2
  478.9 247.3 %all-reduce.6 = (f32[]{:T(128)}, f32[]{:T(128)}) all-reduce(f32[]{:T(128)} %get-tuple-element.434, f32[]{:T(128)} %get-tuple-element.433), channel_id=1, replica_groups=mesh['shift'=4,'cells'=128] {'cells'}, use_global_device_ids=true, to_apply=%region_5.6 | all-reduce | flops 2 | bytes 16 | tf_op jit(solution)/shard_map/psum | solution.py:37
  729.3 174.0 %while.66 = (s32[]{:T(128)}, f32[2,64]{1,0:T(2,128)S(1)}, f32[2,64,1]{1,0,2:T(2,128)S(1)}, f32[7,32,2,64]{3,2,1,0:T(2,128)S(1)}, f32[7,32,2,64,1]{3,2,1,4,0:T(2,...) while((s32[]{:T(128)}, f32[2,64]{1,0:T(2,128)S(1)}, ...), condition=%wide.region_14.15_spmd, body=%wide.region_13.14_spmd.sunk | while | flops 32801 | bytes 507117 | solution.py:33
  923.9 4.3 while.67
  932.0 0.9 concatenate.103
  933.8 248.5 %psum.30 = f32[]{:T(128)} all-reduce(f32[]{:T(128)} %multiply_reduce_fusion.1), channel_id=1, replica_groups=mesh['shift'=4,'cells'=128] {'cells'}, use_global_device_ids=true, to_apply=%region_18.19 | all-reduce | flops 1 | bytes 8 | tf_op jit(solution)/shard_map/psum | solution.py:37
  1183.8 1.3 gather_fusion.1
  1185.1 5.6 fusion.645
  1190.8 2.6 collective-permute-start.5
  1193.3 3.0 collective-permute-start.4
  1196.4 4.6 fusion.680
  1200.9 2.1 scatter_custom_fusion.4
  1203.9 246.2 %psum.31 = f32[]{:T(128)} all-reduce(f32[]{:T(128)} %get-tuple-element.868), channel_id=1, replica_groups=mesh['shift'=4,'cells'=128] {'cells'}, use_global_device_ids=true, to_apply=%region_21.22 | all-reduce | flops 1 | bytes 8 | tf_op jit(solution)/shard_map/psum | solution.py:99
  (1883 shorter events, 413.4 us)
Async XLA Ops:
  1.5 80.3 %collective-permute-start = (f32[1,64,256]{2,1,0:T(8,128)S(1)}, f32[1,64,256]{2,1,0:T(8,128)S(1)}, u32[]{:S(2)}, u32[]{:S(2)}) collective-permute-start(f32[1,64,256]{2,1,0:T(8,128)S(1)} %get-tuple-element.1210), channel_id=1, source_target_pairs={{0,1},{1,2},{2,3},{3,4},{4,5},{5,6},{6,7},{7,8},{8,9},{9,10},{10,1... | collective-permute-start | bytes 196616 | tf_op jit(solution)/shard_map/ppermute | solution.py:17
  6.1 75.8 %collective-permute-start.1 = (f32[1,64,256]{2,1,0:T(8,128)S(1)}, f32[1,64,256]{2,1,0:T(8,128)S(1)}, u32[]{:S(2)}, u32[]{:S(2)}) collective-permute-start(f32[1,64,256]{2,1,0:T(8,128)S(1)} %get-tuple-element.1209), channel_id=1, source_target_pairs={{1,0},{2,1},{3,2},{4,3},{5,4},{6,5},{7,6},{8,7},{9,8},{10,9},{11,1... | collective-permute-start | bytes 196616 | tf_op jit(solution)/shard_map/ppermute | solution.py:19
  15.1 47.9 %all-to-all-start = ((s32[128,2,1]{1,2,0:T(1,128)}), s32[128,2,1]{1,2,0:T(1,128)S(1)}, u32[]{:S(2)}, u32[]{:S(2)}) async-start(s32[128,2,1]{1,2,0:T(1,128)} %bitcast.981), calls=%async_computation | async-start | bytes 131072 | tf_op jit(solution)/shard_map/all_to_all | solution.py:76
  63.0 381.6 %all-to-all-start.1 = ((bf16[256,64,256]{2,1,0:T(8,128)(2,1)}), bf16[256,64,256]{2,1,0:T(8,128)(2,1)}, u32[]{:S(2)}, u32[]{:S(2)}) async-start(bf16[256,64,256]{2,1,0:T(8,128)(2,1)} %scatter_fusion), calls=%async_computation.1 | async-start | bytes 16777216 | tf_op jit(solution)/shard_map/all_to_all | solution.py:74
  295.9 182.2 %collective-permute-start.3 = (f32[1,64,256]{2,1,0:T(8,128)S(1)}, f32[1,64,256]{2,1,0:T(8,128)S(1)}, u32[]{:S(2)}, u32[]{:S(2)}) collective-permute-start(f32[1,64,256]{2,1,0:T(8,128)S(1)} %get-tuple-element.1201), channel_id=1, source_target_pairs={{1,0},{2,1},{3,2},{4,3},{5,4},{6,5},{7,6},{8,7},{9,8},{10,9},{11,1... | collective-permute-start | bytes 196616 | tf_op jit(solution)/shard_map/ppermute | solution.py:19
  298.9 179.2 %collective-permute-start.2 = (f32[1,64,256]{2,1,0:T(8,128)S(1)}, f32[1,64,256]{2,1,0:T(8,128)S(1)}, u32[]{:S(2)}, u32[]{:S(2)}) collective-permute-start(f32[1,64,256]{2,1,0:T(8,128)S(1)} %get-tuple-element.1200), channel_id=1, source_target_pairs={{0,1},{1,2},{2,3},{3,4},{4,5},{5,6},{6,7},{7,8},{8,9},{9,10},{10,1... | collective-permute-start | bytes 196616 | tf_op jit(solution)/shard_map/ppermute | solution.py:17
  444.6 26.4 %all-to-all-start.2 = ((bf16[128,2,64]{2,1,0:T(2,128)(2,1)}), bf16[128,2,64]{2,1,0:T(2,128)(2,1)S(1)}, u32[]{:S(2)}, u32[]{:S(2)}) async-start(bf16[128,2,64]{2,1,0:T(2,128)(2,1)} %bitcast.987), calls=%async_computation.2 | async-start | bytes 131072 | tf_op jit(solution)/shard_map/all_to_all | solution.py:75
  475.6 427.8 %copy-start.6 = (f32[2,64]{1,0:T(2,128)S(1)}, f32[2,64]{1,0:T(2,128)}, u32[]{:S(2)}) copy-start(f32[2,64]{1,0:T(2,128)} %copy-done.5) | copy-start | bytes 1540
  475.6 427.8 %copy-start.78 = (f32[2,64]{1,0:T(2,128)S(1)}, f32[2,64]{1,0:T(2,128)}, u32[]{:S(2)}) copy-start(f32[2,64]{1,0:T(2,128)} %copy-done.77) | copy-start | bytes 1540
  475.6 428.5 %copy-start.4 = (f32[2,64]{1,0:T(2,128)S(1)}, f32[2,64]{1,0:T(2,128)}, u32[]{:S(2)}) copy-start(f32[2,64]{1,0:T(2,128)} %copy-done.3) | copy-start | bytes 1540
  475.6 428.5 %copy-start.76 = (f32[2,64]{1,0:T(2,128)S(1)}, f32[2,64]{1,0:T(2,128)}, u32[]{:S(2)}) copy-start(f32[2,64]{1,0:T(2,128)} %copy-done.75) | copy-start | bytes 1540
  475.6 429.1 %copy-start.74 = (f32[2,64]{1,0:T(2,128)S(1)}, f32[2,64]{1,0:T(2,128)}, u32[]{:S(2)}) copy-start(f32[2,64]{1,0:T(2,128)} %copy-done.73) | copy-start | bytes 1540
  475.6 429.8 %copy-start.72 = (f32[2,64]{1,0:T(2,128)S(1)}, f32[2,64]{1,0:T(2,128)}, u32[]{:S(2)}) copy-start(f32[2,64]{1,0:T(2,128)} %copy-done.71) | copy-start | bytes 1540
  475.6 430.5 %copy-start.70 = (f32[2,64]{1,0:T(2,128)S(1)}, f32[2,64]{1,0:T(2,128)}, u32[]{:S(2)}) copy-start(f32[2,64]{1,0:T(2,128)} %copy-done.69) | copy-start | bytes 1540
  475.7 431.2 %copy-start.68 = (f32[2,64]{1,0:T(2,128)S(1)}, f32[2,64]{1,0:T(2,128)}, u32[]{:S(2)}) copy-start(f32[2,64]{1,0:T(2,128)} %copy-done.67) | copy-start | bytes 1540
  475.7 431.8 %copy-start.66 = (f32[2,64]{1,0:T(2,128)S(1)}, f32[2,64]{1,0:T(2,128)}, u32[]{:S(2)}) copy-start(f32[2,64]{1,0:T(2,128)} %copy-done.65) | copy-start | bytes 1540
  475.7 432.5 %copy-start.64 = (f32[2,64]{1,0:T(2,128)S(1)}, f32[2,64]{1,0:T(2,128)}, u32[]{:S(2)}) copy-start(f32[2,64]{1,0:T(2,128)} %copy-done.63) | copy-start | bytes 1540
  475.7 433.2 %copy-start.62 = (f32[2,64]{1,0:T(2,128)S(1)}, f32[2,64]{1,0:T(2,128)}, u32[]{:S(2)}) copy-start(f32[2,64]{1,0:T(2,128)} %copy-done.61) | copy-start | bytes 1540
  475.7 433.9 %copy-start.60 = (f32[2,64]{1,0:T(2,128)S(1)}, f32[2,64]{1,0:T(2,128)}, u32[]{:S(2)}) copy-start(f32[2,64]{1,0:T(2,128)} %copy-done.59) | copy-start | bytes 1540
  475.7 434.5 %copy-start.58 = (f32[2,64]{1,0:T(2,128)S(1)}, f32[2,64]{1,0:T(2,128)}, u32[]{:S(2)}) copy-start(f32[2,64]{1,0:T(2,128)} %copy-done.57) | copy-start | bytes 1540
  475.7 434.5 %copy-start.80 = (f32[2,64]{1,0:T(2,128)S(1)}, f32[2,64]{1,0:T(2,128)}, u32[]{:S(2)}) copy-start(f32[2,64]{1,0:T(2,128)} %copy-done.79) | copy-start | bytes 1540
  475.7 434.5 %copy-start.56 = (f32[2,64]{1,0:T(2,128)S(1)}, f32[2,64]{1,0:T(2,128)}, u32[]{:S(2)}) copy-start(f32[2,64]{1,0:T(2,128)} %copy-done.55) | copy-start | bytes 1540
  475.7 435.2 %copy-start.42 = (f32[2,64]{1,0:T(2,128)S(1)}, f32[2,64]{1,0:T(2,128)}, u32[]{:S(2)}) copy-start(f32[2,64]{1,0:T(2,128)} %copy-done.41) | copy-start | bytes 1540
  475.7 435.2 %copy-start.54 = (f32[2,64]{1,0:T(2,128)S(1)}, f32[2,64]{1,0:T(2,128)}, u32[]{:S(2)}) copy-start(f32[2,64]{1,0:T(2,128)} %copy-done.53) | copy-start | bytes 1540
  475.8 435.8 %copy-start.40 = (f32[2,64]{1,0:T(2,128)S(1)}, f32[2,64]{1,0:T(2,128)}, u32[]{:S(2)}) copy-start(f32[2,64]{1,0:T(2,128)} %copy-done.39) | copy-start | bytes 1540
  475.8 435.8 %copy-start.52 = (f32[2,64]{1,0:T(2,128)S(1)}, f32[2,64]{1,0:T(2,128)}, u32[]{:S(2)}) copy-start(f32[2,64]{1,0:T(2,128)} %copy-done.51) | copy-start | bytes 1540
  475.8 436.5 %copy-start.38 = (f32[2,64]{1,0:T(2,128)S(1)}, f32[2,64]{1,0:T(2,128)}, u32[]{:S(2)}) copy-start(f32[2,64]{1,0:T(2,128)} %copy-done.37) | copy-start | bytes 1540
  475.8 436.5 %copy-start.50 = (f32[2,64]{1,0:T(2,128)S(1)}, f32[2,64]{1,0:T(2,128)}, u32[]{:S(2)}) copy-start(f32[2,64]{1,0:T(2,128)} %copy-done.49) | copy-start | bytes 1540
  475.8 437.2 %copy-start.36 = (f32[2,64]{1,0:T(2,128)S(1)}, f32[2,64]{1,0:T(2,128)}, u32[]{:S(2)}) copy-start(f32[2,64]{1,0:T(2,128)} %copy-done.35) | copy-start | bytes 1540
  475.8 437.2 %copy-start.48 = (f32[2,64]{1,0:T(2,128)S(1)}, f32[2,64]{1,0:T(2,128)}, u32[]{:S(2)}) copy-start(f32[2,64]{1,0:T(2,128)} %copy-done.47) | copy-start | bytes 1540
  475.8 437.8 %copy-start.34 = (f32[2,64]{1,0:T(2,128)S(1)}, f32[2,64]{1,0:T(2,128)}, u32[]{:S(2)}) copy-start(f32[2,64]{1,0:T(2,128)} %copy-done.33) | copy-start | bytes 1540
  475.8 437.8 %copy-start.46 = (f32[2,64]{1,0:T(2,128)S(1)}, f32[2,64]{1,0:T(2,128)}, u32[]{:S(2)}) copy-start(f32[2,64]{1,0:T(2,128)} %copy-done.45) | copy-start | bytes 1540
  475.8 438.5 %copy-start.32 = (f32[2,64]{1,0:T(2,128)S(1)}, f32[2,64]{1,0:T(2,128)}, u32[]{:S(2)}) copy-start(f32[2,64]{1,0:T(2,128)} %copy-done.31) | copy-start | bytes 1540
  475.8 438.5 %copy-start.44 = (f32[2,64]{1,0:T(2,128)S(1)}, f32[2,64]{1,0:T(2,128)}, u32[]{:S(2)}) copy-start(f32[2,64]{1,0:T(2,128)} %copy-done.43) | copy-start | bytes 1540
  475.9 439.2 %copy-start.30 = (f32[2,64]{1,0:T(2,128)S(1)}, f32[2,64]{1,0:T(2,128)}, u32[]{:S(2)}) copy-start(f32[2,64]{1,0:T(2,128)} %copy-done.29) | copy-start | bytes 1540
  475.9 439.8 %copy-start.28 = (f32[2,64]{1,0:T(2,128)S(1)}, f32[2,64]{1,0:T(2,128)}, u32[]{:S(2)}) copy-start(f32[2,64]{1,0:T(2,128)} %copy-done.27) | copy-start | bytes 1540
  475.9 440.5 %copy-start.26 = (f32[2,64]{1,0:T(2,128)S(1)}, f32[2,64]{1,0:T(2,128)}, u32[]{:S(2)}) copy-start(f32[2,64]{1,0:T(2,128)} %copy-done.25) | copy-start | bytes 1540
  475.9 441.2 %copy-start.24 = (f32[2,64]{1,0:T(2,128)S(1)}, f32[2,64]{1,0:T(2,128)}, u32[]{:S(2)}) copy-start(f32[2,64]{1,0:T(2,128)} %copy-done.23) | copy-start | bytes 1540
  475.9 441.9 %copy-start.22 = (f32[2,64]{1,0:T(2,128)S(1)}, f32[2,64]{1,0:T(2,128)}, u32[]{:S(2)}) copy-start(f32[2,64]{1,0:T(2,128)} %copy-done.21) | copy-start | bytes 1540
  475.9 442.5 %copy-start.20 = (f32[2,64]{1,0:T(2,128)S(1)}, f32[2,64]{1,0:T(2,128)}, u32[]{:S(2)}) copy-start(f32[2,64]{1,0:T(2,128)} %copy-done.19) | copy-start | bytes 1540
  475.9 443.2 %copy-start.18 = (f32[2,64]{1,0:T(2,128)S(1)}, f32[2,64]{1,0:T(2,128)}, u32[]{:S(2)}) copy-start(f32[2,64]{1,0:T(2,128)} %copy-done.17) | copy-start | bytes 1540
  475.9 443.8 %copy-start.16 = (f32[2,64]{1,0:T(2,128)S(1)}, f32[2,64]{1,0:T(2,128)}, u32[]{:S(2)}) copy-start(f32[2,64]{1,0:T(2,128)} %copy-done.15) | copy-start | bytes 1540
  475.9 444.5 %copy-start.14 = (f32[2,64]{1,0:T(2,128)S(1)}, f32[2,64]{1,0:T(2,128)}, u32[]{:S(2)}) copy-start(f32[2,64]{1,0:T(2,128)} %copy-done.13) | copy-start | bytes 1540
  475.9 445.2 %copy-start.12 = (f32[2,64]{1,0:T(2,128)S(1)}, f32[2,64]{1,0:T(2,128)}, u32[]{:S(2)}) copy-start(f32[2,64]{1,0:T(2,128)} %copy-done.11) | copy-start | bytes 1540
  476.0 445.9 %copy-start.10 = (f32[2,64]{1,0:T(2,128)S(1)}, f32[2,64]{1,0:T(2,128)}, u32[]{:S(2)}) copy-start(f32[2,64]{1,0:T(2,128)} %copy-done.9) | copy-start | bytes 1540
  476.0 447.1 %copy-start.8 = (f32[2,64]{1,0:T(2,128)S(1)}, f32[2,64]{1,0:T(2,128)}, u32[]{:S(2)}) copy-start(f32[2,64]{1,0:T(2,128)} %copy-done.7) | copy-start | bytes 1540
  1190.8 12.3 collective-permute-start.5
  1193.3 9.8 collective-permute-start.4
  (43 other events, 7854.8 us)
where the time goes:
time: 1460 us; the launch traced here: 1450 us
  blocking collectives  742 us (51%)
  other arithmetic  399 us (27%)
  waiting for transfers between devices  151 us (10%)
  starting transfers between devices  66.2 us (5%)
  local copies, waits for them, and re-layouts  64.2 us (4%)
  matrix products  20.4 us (1%)
    psum x2, blocking collectives, norm_sum(): return lax.psum(jnp.sum(residual * smoothed), 'cells')  496 us
    while x434, other arithmetic  305 us
    psum x1, blocking collectives, on_device(): alpha = norm_now / lax.psum(jnp.sum(direction * image), 'cells')  246 us
    all_to_all x1, waiting for transfers between devices, on_device(): lax.all_to_all(send_blocks, 'cells', split_axis=0, concat_axis=0, tiled=T...  142 us
    unnamed x116, other arithmetic  38.9 us
  transfers between devices with their start and end apart: 9, of which 2 were waited for; matrix products, arithmetic and copies ran while one was open for 18% of the time, Pallas kernels for 0%

commit v1 on v0

v1 whole, which is shorter than its diff:
```python
import functools

import jax
import jax.numpy as jnp
from jax import lax
from jax.experimental import pallas as pl
from jax.experimental.pallas import tpu as pltpu
from jax.sharding import PartitionSpec as P

F32 = jnp.float32
BF16 = jnp.bfloat16
LANES = 128
GROUP = 16
ALONG_Y = 4
LARGEST = 32767.0


def nt(a, b):
    return lax.dot_general(a, b, (((1,), (1,)), ((), ())), preferred_element_type=F32)


def nn(a, b):
    return lax.dot_general(a, b, (((1,), (0,)), ((), ())), preferred_element_type=F32)


def iota(shape, dim):
    return lax.broadcasted_iota(jnp.int32, shape, dim)


def harmonic(first, second):
    return 2.0 * first * second / (first + second)


def up(v, k, axis=0):
    return pltpu.roll(v, k, axis)


def down(v, k, axis=0):
    return pltpu.roll(v, v.shape[axis] - k, axis)


def fold(v):
    total = v[0:8]
    for i in range(8, v.shape[0], 8):
        total = total + v[i : i + 8]
    return total


def split(v):
    high = v.astype(BF16)
    return high, (v - high.astype(F32)).astype(BF16)


def picked(weights, v):
    high, low = split(v)
    return nn(weights, high) + nn(weights, low)


def whole_sum(v):
    return jnp.sum(jnp.sum(v, axis=0, keepdims=True), axis=1, keepdims=True)


def kernel(
    n,
    perm_ref,
    storage_ref,
    right_ref,
    coupling_ref,
    gains_ref,
    target_ref,
    column_ref,
    sol_ref,
    res_ref,
    mat,
    coef,
    alpha_ref,
    gamma_ref,
    pivot_ref,
    perm_halo,
    halo_send,
    halo_recv,
    hot_send,
    hot_recv,
    data_send,
    data_recv,
    meta_send,
    meta_recv,
    take_ref,
    give_ref,
    gather_ref,
    scatter_ref,
    gm_ref,
    mat_sem,
    halo_sem,
    hot_sem,
    data_sem,
    meta_sem,
):
    me = lax.axis_index("cells")
    chip = me // 2
    core = me % 2
    chips = n // 2
    along_z = chips // ALONG_Y
    z_here = chip // ALONG_Y
    y_here = chip % ALONG_Y
    sibling = chip * 2 + (1 - core)
    left = lax.rem(me + n - 1, n)
    right = lax.rem(me + 1, n)
    height = coef.shape[1]
    half = height // 2
    comp = target_ref.shape[1]
    slots = chips * 8
    steps = alpha_ref.shape[0]

    load = pltpu.make_async_copy(coupling_ref, mat, mat_sem)
    load.start()

    def greet(device):
        pl.semaphore_signal(
            pltpu.get_barrier_semaphore(),
            inc=1,
            device_id={"cells": device},
            device_id_type=pl.DeviceIdType.MESH,
        )

    def send(src, dst, sems, device):
        copy = pltpu.make_async_remote_copy(
            src_ref=src,
            dst_ref=dst,
            send_sem=sems.at[0],
            recv_sem=sems.at[1],
            device_id={"cells": device},
            device_id_type=pl.DeviceIdType.MESH,
        )
        copy.start()
        return copy

    def await_bytes(ref, sem):
        pltpu.make_async_copy(ref, ref, sem).wait()

    def to_chips(act):
        def plane(j, carry):
            away = along_z // 2 + (j % 2) * (j // 2) - (1 - j % 2) * (j // 2)
            z = lax.rem(z_here + away, along_z)
            for across in (2, 1, 3, 0):
                act(z * ALONG_Y + lax.rem(y_here + across, ALONG_Y))
            return carry

        lax.fori_loop(1, along_z, plane, 0)
        for across in (2, 1, 3):
            act(z_here * ALONG_Y + lax.rem(y_here + across, ALONG_Y))

    to_chips(lambda q: greet(q * 2 + core))
    greet(left)
    greet(right)
    greet(sibling)

    lane = iota((height, LANES), 1)
    row = iota((height, LANES), 0)
    first_layer = lane < 64
    perm = perm_ref[...].T
    r0 = right_ref[...].T

    t_all = jnp.broadcast_to(target_ref[...].astype(F32), (LANES, LANES))
    c_all = jnp.broadcast_to(column_ref[...].astype(F32), (LANES, LANES))
    t_side = t_all.T
    c_side = c_all.T
    sq_row = iota((LANES, LANES), 0)
    sq_lane = iota((LANES, LANES), 1)
    same = t_all == t_side
    rank_all = jnp.sum(jnp.where(same & (sq_row < sq_lane), 1.0, 0.0), axis=0, keepdims=True)
    rank_side = jnp.sum(jnp.where(same & (sq_lane < sq_row), 1.0, 0.0), axis=1, keepdims=True)

    def parts(target, rank):
        t = target.astype(jnp.int32)
        return lax.shift_right_logical(t, 1), t & 1, rank.astype(jnp.int32)

    q_all, core_all, rank_all = parts(t_all[0:1], rank_all)
    q_side, core_side, rank_side = parts(t_side[:, 0:1], rank_side)
    out_row = q_all * 8 + core_all * 4 + rank_all * 2
    give_ref[...] = jnp.where(
        iota((slots, 2 * comp), 0) == jnp.concatenate([out_row, out_row + 1], axis=1), 1.0, 0.0
    ).astype(BF16)
    in_row = jnp.where(core_side == core, 0, slots) + q_side * 8 + core * 4 + rank_side * 2
    take_ref[...] = jnp.where(
        iota((2 * comp, 2 * slots), 1) == jnp.concatenate([in_row, in_row + 1], axis=0), 1.0, 0.0
    ).astype(BF16)
    weight = jnp.where(core_all == 1, 4.0, 1.0) * jnp.where(rank_all == 1, 2.0, 1.0)
    hot = jnp.where(c_side.astype(jnp.int32) == sq_lane, 1.0, 0.0).astype(BF16)
    codes = nn(jnp.where(iota((chips, comp), 0) == q_all, weight, 0.0).astype(BF16), hot)
    for q in range(chips):
        hot_send[q] = codes[q : q + 1]

    pl.semaphore_wait(pltpu.get_barrier_semaphore(), chips + 2)

    hot_recv[0, pl.ds(chip, 1)] = hot_send[pl.ds(chip, 1)]
    to_chips(lambda q: send(hot_send.at[q], hot_recv.at[0, chip], hot_sem.at[0], q * 2 + core))
    perm_right = send(
        perm_ref.at[pl.ds(64, 64)], perm_halo.at[pl.ds(0, 64)], halo_sem.at[0], right
    )
    perm_left = send(
        perm_ref.at[pl.ds(0, 64)], perm_halo.at[pl.ds(64, 64)], halo_sem.at[1], left
    )

    trans_in = harmonic(perm, up(perm, 64, 1))
    y_low = jnp.where((lane & 63) == 0, 0.0, harmonic(perm, up(perm, 1, 1)))
    y_high = down(y_low, 1, 1)
    z_low = jnp.where(row == 0, 0.0, harmonic(perm, up(perm, 1)))
    z_high = down(z_low, 1)
    coef[1] = trans_in
    coef[3] = y_low
    coef[4] = y_high
    coef[5] = z_low
    coef[6] = z_high
    part_diag = storage_ref[...].T + trans_in + y_low + y_high + z_low + z_high

    perm_right.wait_recv()
    perm_left.wait_recv()
    trans_out = harmonic(perm, perm_halo[...].T)
    outside = (first_layer & (me == 0)) | (jnp.logical_not(first_layer) & (me == n - 1))
    trans_out = jnp.where(outside, 0.0, trans_out)
    coef[2] = trans_out
    coef[0] = part_diag + trans_out

    a = -z_low
    b = coef[0]
    for s in range(steps):
        k = 1 << s
        rb = 1.0 / b
        scaled = -a * rb
        alpha = -a * up(rb, k)
        gamma = down(scaled, k)
        alpha_ref[s] = alpha
        gamma_ref[s] = gamma
        b = b + down(a * scaled, k) + alpha * a
        if s + 1 < steps:
            a = alpha * up(a, k)
    pivot_ref[...] = 1.0 / b

    def precondition(d):
        for s in range(steps):
            k = 1 << s
            d = d + alpha_ref[s] * up(d, k) + gamma_ref[s] * down(d, k)
        return d * pivot_ref[...]

    def start_halo(v, which):
        top, bottom = v[:half], v[half:]
        low = iota(top.shape, 1) < 64
        halo_send[which, 0] = jnp.where(low, up(top, 64, 1), bottom)
        halo_send[which, 1] = jnp.where(low, top, up(bottom, 64, 1))
        return (
            send(
                halo_send.at[which, 0],
                halo_recv.at[which, 0],
                halo_sem.at[2 + 2 * which],
                right,
            ),
            send(
                halo_send.at[which, 1],
                halo_recv.at[which, 1],
                halo_sem.at[3 + 2 * which],
                left,
            ),
        )

    def stencil(v, which, copies):
        part = (
            coef[0] * v
            - coef[1] * up(v, 64, 1)
            - coef[3] * up(v, 1, 1)
            - coef[4] * down(v, 1, 1)
            - coef[5] * up(v, 1)
            - coef[6] * down(v, 1)
        )
        for copy in copies:
            copy.wait_recv()
        before, after = halo_recv[which, 0], halo_recv[which, 1]
        low = iota(before.shape, 1) < 64
        halo = jnp.concatenate(
            [
                jnp.where(low, before, up(after, 64, 1)),
                jnp.where(low, up(before, 64, 1), after),
            ],
            axis=0,
        )
        return part - coef[2] * halo

    def wells(rows):
        chosen = rows.astype(BF16)
        backs, dot = [], jnp.zeros((8, LANES), F32)
        for g in range(comp // GROUP):
            block = mat[pl.ds(g * GROUP * 64, GROUP * 64), :]
            y = nt(chosen[g * GROUP : (g + 1) * GROUP], block)
            u = (y * gm_ref[pl.ds(g * GROUP, GROUP), :]).astype(BF16)
            backs.append(nn(u, block))
            both = fold(y * u.astype(F32))
            for i in range(0, GROUP * 64, LANES):
                dot = dot + both[:, i : i + LANES]
        return jnp.concatenate(backs, axis=0), dot

    def start_exchange(which, v, sums):
        largest = jnp.maximum(jnp.max(jnp.max(jnp.abs(v), axis=0, keepdims=True), axis=1, keepdims=True), 1e-30)
        fixed = jnp.round(v * (LARGEST / largest))
        data_send[which] = fixed.astype(jnp.int32).astype(jnp.int16).reshape(chips, 8, LANES)
        at = iota((1, LANES), 1)
        meta = jnp.where(at == 0, largest * (1.0 / LARGEST), 0.0)
        for i, term in enumerate(sums):
            meta = jnp.where(at == i + 1, whole_sum(term), meta)
        meta_send[which] = meta
        data_recv[which, 0, pl.ds(chip, 1)] = data_send[which, pl.ds(chip, 1)]
        meta_recv[which, 0, pl.ds(chip, 1)] = meta[None]

        def act(q):
            send(data_send.at[which, q], data_recv.at[which, 0, chip], data_sem.at[which, 0], q * 2 + core)
            send(meta_send.at[which], meta_recv.at[which, 0, chip], meta_sem.at[which, 0], q * 2 + core)

        to_chips(act)

    def swap(ref, sems):
        await_bytes(ref.at[0, pl.ds(0, chips - 1)], sems.at[0, 1])
        return send(ref.at[0], ref.at[1], sems.at[1], sibling)

    def finish_exchange(which, weights):
        data = data_recv.at[which]
        meta = meta_recv.at[which]
        data_swap = swap(data, data_sem.at[which])
        meta_swap = swap(meta, meta_sem.at[which])

        def received(side):
            unit = meta[side][:, :, 0:1]
            v = data[side].astype(jnp.int32).astype(F32) * unit
            return picked(weights[:, side * slots : (side + 1) * slots], v.reshape(slots, LANES))

        total = received(0)
        data_swap.wait_recv()
        meta_swap.wait_recv()
        total = total + received(1)
        sums = jnp.sum(meta[0], axis=0) + jnp.sum(meta[1], axis=0)
        return total, sums

    def drain(ref_one, ref_all, sems):
        await_bytes(ref_all.at[0, pl.ds(0, chips - 1)], sems.at[0, 0])
        await_bytes(ref_one.at[0], sems.at[1, 0])

    def columns_of(v):
        return jnp.concatenate([v[:half].T, v[half:].T], axis=0)

    def side_by_side(v):
        return jnp.concatenate([v[:comp], v[comp:]], axis=1)

    def stacked(v):
        return jnp.concatenate([v[:, :half], v[:, half:]], axis=0)

    z0 = precondition(r0)

    hot_swap = swap(hot_recv, hot_sem)
    z0_cols = columns_of(z0)
    z0_high, z0_low = split(z0_cols)
    hot_swap.wait_recv()
    codes = jnp.concatenate([hot_recv[0, :, 0, :], hot_recv[1, :, 0, :]], axis=0).astype(BF16)
    r = iota((slots, 2 * chips), 0)
    source = lax.shift_right_logical(r, 3) + jnp.where(
        (lax.shift_right_logical(r, 2) & 1) == core, 0, chips
    )
    spread = jnp.where(iota((slots, 2 * chips), 1) == source, 1.0, 0.0).astype(BF16)
    r = iota((slots, LANES), 0)
    bit = lax.shift_right_logical(r, 1) & 1
    asked = nn(spread, codes).astype(jnp.int32)
    asked = (lax.shift_right_logical(asked, 2 * core + bit) & 1).astype(F32)
    upper = (r & 1) == 1
    gather_ref[...] = jnp.concatenate(
        [jnp.where(upper, 0.0, asked), jnp.where(upper, asked, 0.0)], axis=1
    ).astype(BF16)
    start_exchange(0, nn(gather_ref[...], z0_high) + nn(gather_ref[...], z0_low), [])
    halo0 = start_halo(z0, 0)

    r = iota((2 * chips, 2 * slots), 1)
    spread = jnp.where(
        lax.shift_right_logical(r, 3) == iota((2 * chips, 2 * slots), 0), 1.0, 0.0
    ).astype(BF16)
    asked = nn(codes.astype(F32).T.astype(BF16), spread).astype(jnp.int32)
    r = iota((LANES, 2 * slots), 1)
    bit = lax.shift_right_logical(r, 1) & 1
    mine = (lax.shift_right_logical(r, 2) & 1) == core
    asked = (lax.shift_right_logical(asked, 2 * core + bit) & 1).astype(F32)
    asked = jnp.where(mine, asked, 0.0)
    upper = (r & 1) == 1
    scatter_ref[...] = jnp.concatenate(
        [jnp.where(upper, 0.0, asked), jnp.where(upper, asked, 0.0)], axis=0
    ).astype(BF16)

    gains = gains_ref[...].astype(F32).T.astype(BF16)
    wide = GROUP * 64
    spread = jnp.where((iota((64, wide), 1) & 63) == iota((64, wide), 0), 1.0, 0.0)
    gm_ref[...] = jnp.where(
        (iota((comp, wide), 0) & (GROUP - 1)) == lax.shift_right_logical(iota((comp, wide), 1), 6),
        nn(gains, spread.astype(BF16)),
        0.0,
    )
    s0 = stencil(z0, 0, halo0)
    rz_part = fold(r0 * z0)
    zs_part = fold(z0 * s0)
    load.wait()

    rows, _ = finish_exchange(0, take_ref)
    rows0 = side_by_side(rows)
    back, yu = wells(rows0)
    start_exchange(1, picked(give_ref[...], stacked(back)), [rz_part, zs_part + yu])
    added, sums = finish_exchange(1, scatter_ref)
    rz0, g00 = sums[:, 1:2], sums[:, 2:3]
    alpha0 = rz0 / g00
    w0 = jnp.concatenate([added[:LANES].T, added[LANES:].T], axis=0)
    r1 = r0 - alpha0 * (s0 + w0)
    z1 = precondition(r1)

    start_exchange(2, picked(gather_ref[...], columns_of(z1)), [fold(r1 * z1)])
    halo1 = start_halo(z1, 1)
    s1 = stencil(z1, 1, halo1)
    rows, sums = finish_exchange(2, take_ref)
    fresh = sums[:, 1:2]
    beta = fresh / rz0
    back, yu = wells(side_by_side(rows) + beta * rows0)
    d1 = z1 + beta * z0
    image = s1 + beta * s0
    start_exchange(3, picked(give_ref[...], stacked(back)), [fold(d1 * image) + yu])
    added, sums = finish_exchange(3, scatter_ref)
    alpha1 = fresh / sums[:, 1:2]
    sol_ref[...] = (alpha0 * z0 + alpha1 * d1).T
    w1 = jnp.concatenate([added[:LANES].T, added[LANES:].T], axis=0)
    res_ref[...] = (r1 - alpha1 * (image + w1)).T

    for copy in (perm_right, perm_left, *halo0, *halo1):
        copy.wait_send()
    drain(hot_recv, hot_recv, hot_sem)
    for i in range(4):
        drain(data_recv.at[i], data_recv.at[i], data_sem.at[i])
        drain(meta_recv.at[i], meta_recv.at[i], meta_sem.at[i])


def on_device(perm, storage, right_side, coupling, gains, well_target, well_column):
    n = lax.axis_size("cells")
    chips = n // 2
    comp, perforations, height = coupling.shape
    slots = chips * 8
    shape = perm.shape
    columns = shape[0] * shape[1]
    steps = (height - 1).bit_length()

    def flat(x):
        return x.reshape(columns, height)

    vmem = pl.BlockSpec(memory_space=pltpu.VMEM)
    dma = pltpu.SemaphoreType.DMA
    sol, res = pl.pallas_call(
        functools.partial(kernel, n),
        out_shape=[jax.ShapeDtypeStruct((columns, height), F32)] * 2,
        in_specs=[vmem] * 3 + [pl.BlockSpec(memory_space=pl.ANY)] + [vmem] * 3,
        out_specs=[vmem] * 2,
        scratch_shapes=[
            pltpu.VMEM((comp * perforations, height), BF16),
            pltpu.VMEM((7, height, LANES), F32),
            pltpu.VMEM((steps, height, LANES), F32),
            pltpu.VMEM((steps, height, LANES), F32),
            pltpu.VMEM((height, LANES), F32),
            pltpu.VMEM((columns, height), F32),
            pltpu.VMEM((2, 2, height // 2, LANES), F32),
            pltpu.VMEM((2, 2, height // 2, LANES), F32),
            pltpu.VMEM((chips, 1, LANES), F32),
            pltpu.VMEM((2, chips, 1, LANES), F32),
            pltpu.VMEM((4, chips, 8, LANES), jnp.int16),
            pltpu.VMEM((4, 2, chips, 8, LANES), jnp.int16),
            pltpu.VMEM((4, 1, LANES), F32),
            pltpu.VMEM((4, 2, chips, 1, LANES), F32),
            pltpu.VMEM((2 * comp, 2 * slots), BF16),
            pltpu.VMEM((slots, 2 * comp), BF16),
            pltpu.VMEM((slots, 2 * LANES), BF16),
            pltpu.VMEM((2 * LANES, 2 * slots), BF16),
            pltpu.VMEM((comp, GROUP * perforations), F32),
            dma,
            dma((6, 2)),
            dma((2, 2)),
            dma((4, 2, 2)),
            dma((4, 2, 2)),
        ],
        compiler_params=pltpu.CompilerParams(
            collective_id=0, has_side_effects=True, vmem_limit_bytes=48 * 1024 * 1024
        ),
    )(
        flat(perm),
        flat(storage),
        flat(right_side),
        coupling.reshape(comp * perforations, height),
        gains.T,
        well_target.reshape(1, comp),
        well_column.reshape(1, comp),
    )
    return sol.reshape(shape), res.reshape(shape)


def solution(mesh):
    cells = P(("shift", "cells"), None, None)
    in_specs = (
        cells,
        cells,
        cells,
        P("cells", None, None),
        P("cells", None),
        P("cells", None),
        P("cells"),
    )
    return jax.shard_map(
        on_device, mesh=mesh, in_specs=in_specs, out_specs=(cells, cells), check_vma=False
    )
```

time: 1460 us -> 93.6 us (0.06)
  blocking collectives: 742 us -> 0 us
  other arithmetic: 399 us -> 0 us
  waiting for transfers between devices: 151 us -> 0 us
  Pallas kernels: 0 us -> 84.4 us
  starting transfers between devices: 66.2 us -> 0 us
  local copies, waits for them, and re-layouts: 64.2 us -> 8.23 us
  matrix products: 20.4 us -> 0 us
    psum x3 -> x0, blocking collectives: 742 us -> none  [the longest x2 496 us: norm_sum(): return lax.psum(jnp.sum(residual * smoothed), 'cells')]
    while x434 -> x0, other arithmetic: 305 us -> none
    all_to_all x3 -> x0, waiting for transfers between devices: 151 us -> none  [the longest x1 142 us: on_device(): lax.all_to_all(send_blocks, 'cells', split_axis=0, concat_axis=0, tiled=T...]
    pallas_call x0 -> x1, Pallas kernels: none -> 84.4 us  [on_device(): pl.pallas_call(functools.partial(kernel, n), out_shape=[jax.ShapeDtypeStr...]
    all_to_all x3 -> x0, starting transfers between devices: 45 us -> none  [the longest x1 16.7 us: on_device(): lax.all_to_all(send_blocks, 'cells', split_axis=0, concat_axis=0, tiled=T...]
    unnamed x116 -> x0, other arithmetic: 38.9 us -> none
    div x35 -> x0, other arithmetic: 23 us -> none  [the longest x32 20.8 us: precondition(): lax.linalg.tridiagonal_solve(lower, diagonal, upper, values[..., None])]
    scatter x3 -> x0, local copies, waits for them, and re-layouts: 21.9 us -> none  [the longest x1 19.3 us: on_device(): jnp.zeros((total_slots, perforations, width_z), jnp.bfloat16)]
  transfers between devices with their start and end apart: 9 -> 0, of which waited for: 2 -> 0; matrix products, arithmetic and copies ran while one was open for 18% -> 0% of each run, Pallas kernels for 0% -> 0%
where the time goes in v1:
time: 93.6 us; the launch traced here: 93.3 us
  Pallas kernels  84.4 us (90%)
  local copies, waits for them, and re-layouts  8.23 us (9%)
    pallas_call x1, Pallas kernels, on_device(): pl.pallas_call(functools.partial(kernel, n), out_shape=[jax.ShapeDtypeStr...  84.4 us
    unnamed x16, local copies, waits for them, and re-layouts  8.23 us

profile of v1, /device:TPU:1, one launch (start us, length us, event | category | flops | bytes accessed | tf_op | source)
XLA Modules:
  0.0 93.3 jit_solution(5639157329730514710)
XLA Ops:
  0.6 0.0 copy-start
  0.6 2.2 %copy-done = bf16[128,64,256]{2,1,0:T(8,128)(2,1)S(1)} copy-done((bf16[128,64,256]{2,1,0:T(8,128)(2,1)S(1)}, bf16[128,64,256]{2,1,0:T(8,128)(2,1)}, u32[]{:S(2)}) %copy-start) | copy-done | bytes 4194328
  2.8 0.0 copy-start.1
  2.8 0.9 copy-done.1
  3.7 0.0 copy-start.2
  3.7 0.9 copy-done.2
  4.6 0.0 copy-start.3
  4.6 0.9 copy-done.3
  5.5 0.0 copy-start.4
  5.5 0.7 copy-done.4
  6.3 0.0 copy-start.5
  6.3 0.7 copy-done.5
  6.9 0.0 copy-start.6
  6.9 0.7 copy-done.6
  7.6 84.4 %shard_map.86 = (f32[128,256]{1,0:T(8,128)S(1)}, f32[128,256]{1,0:T(8,128)S(1)}) custom-call(f32[128,256]{1,0:T(8,128)S(1)} %bitcast.10, f32[128,256]{1,0:T(8,128)S(1)} %bitcast.11, f32[128,256]{1,0:T(8,128)S(1)} %bitcast.12, bf16[8192,256]{1,0:T(8,128)(2,1)S(1)} %bitcast.9, bf16[64,128]{1,0:T(8,128)(2,1)S(1)} %bitcast.15, s32[1,128]{1,0:T(1,128)S(1)} %bitcast.16, ...), custom_call_target="tpu_custom_call" | custom-call | tf_op jit(solution)/shard_map/pallas_call | solution.py:454
  92.0 0.7 copy.11
  92.7 0.7 copy.12
Async XLA Ops:
  0.6 2.2 %copy-start = (bf16[128,64,256]{2,1,0:T(8,128)(2,1)S(1)}, bf16[128,64,256]{2,1,0:T(8,128)(2,1)}, u32[]{:S(2)}) copy-start(bf16[128,64,256]{2,1,0:T(8,128)(2,1)} %param.10) | copy-start | bytes 12582916
  2.8 0.9 copy-start.1
  3.7 0.9 copy-start.2
  4.6 0.9 copy-start.3
  5.5 0.7 copy-start.4
  6.3 0.7 copy-start.5
  6.9 0.7 copy-start.6

commit v2 on v1

--- a/solution.py
+++ b/solution.py
@@ -62,15 +62,21 @@
 
 def kernel(
     n,
+    perm_hbm,
+    storage_hbm,
+    right_hbm,
+    coupling_hbm,
+    gains_hbm,
+    target_hbm,
+    column_hbm,
+    sol_ref,
+    res_ref,
     perm_ref,
     storage_ref,
     right_ref,
-    coupling_ref,
     gains_ref,
     target_ref,
     column_ref,
-    sol_ref,
-    res_ref,
     mat,
     coef,
     alpha_ref,
@@ -90,7 +96,8 @@
     gather_ref,
     scatter_ref,
     gm_ref,
-    mat_sem,
+    mat_t,
+    load_sem,
     halo_sem,
     hot_sem,
     data_sem,
@@ -112,8 +119,22 @@
     slots = chips * 8
     steps = alpha_ref.shape[0]
 
-    load = pltpu.make_async_copy(coupling_ref, mat, mat_sem)
-    load.start()
+    loads = [
+        pltpu.make_async_copy(src, dst, load_sem.at[i])
+        for i, (src, dst) in enumerate(
+            [
+                (target_hbm, target_ref),
+                (column_hbm, column_ref),
+                (perm_hbm, perm_ref),
+                (right_hbm, right_ref),
+                (storage_hbm, storage_ref),
+                (gains_hbm, gains_ref),
+                (coupling_hbm, mat),
+            ]
+        )
+    ]
+    for load in loads:
+        load.start()
 
     def greet(device):
         pl.semaphore_signal(
@@ -155,6 +176,8 @@
     greet(right)
     greet(sibling)
 
+    for load in loads[:6]:
+        load.wait()
     lane = iota((height, LANES), 1)
     row = iota((height, LANES), 0)
     first_layer = lane < 64
@@ -190,6 +213,11 @@
     codes = nn(jnp.where(iota((chips, comp), 0) == q_all, weight, 0.0).astype(BF16), hot)
     for q in range(chips):
         hot_send[q] = codes[q : q + 1]
+
+    loads[6].wait()
+    for g in range(comp // GROUP):
+        rows = pl.ds(g * GROUP * 64, GROUP * 64)
+        mat_t[:, rows] = mat[rows, :].T
 
     pl.semaphore_wait(pltpu.get_barrier_semaphore(), chips + 2)
 
@@ -290,7 +318,7 @@
         backs, dot = [], jnp.zeros((8, LANES), F32)
         for g in range(comp // GROUP):
             block = mat[pl.ds(g * GROUP * 64, GROUP * 64), :]
-            y = nt(chosen[g * GROUP : (g + 1) * GROUP], block)
+            y = nn(chosen[g * GROUP : (g + 1) * GROUP], mat_t[:, pl.ds(g * GROUP * 64, GROUP * 64)])
             u = (y * gm_ref[pl.ds(g * GROUP, GROUP), :]).astype(BF16)
             backs.append(nn(u, block))
             both = fold(y * u.astype(F32))
@@ -400,8 +428,6 @@
     s0 = stencil(z0, 0, halo0)
     rz_part = fold(r0 * z0)
     zs_part = fold(z0 * s0)
-    load.wait()
-
     rows, _ = finish_exchange(0, take_ref)
     rows0 = side_by_side(rows)
     back, yu = wells(rows0)
@@ -454,9 +480,15 @@
     sol, res = pl.pallas_call(
         functools.partial(kernel, n),
         out_shape=[jax.ShapeDtypeStruct((columns, height), F32)] * 2,
-        in_specs=[vmem] * 3 + [pl.BlockSpec(memory_space=pl.ANY)] + [vmem] * 3,
+        in_specs=[pl.BlockSpec(memory_space=pl.ANY)] * 7,
         out_specs=[vmem] * 2,
         scratch_shapes=[
+            pltpu.VMEM((columns, height), F32),
+            pltpu.VMEM((columns, height), F32),
+            pltpu.VMEM((columns, height), F32),
+            pltpu.VMEM((perforations, comp), BF16),
+            pltpu.VMEM((1, comp), jnp.int32),
+            pltpu.VMEM((1, comp), jnp.int32),
             pltpu.VMEM((comp * perforations, height), BF16),
             pltpu.VMEM((7, height, LANES), F32),
             pltpu.VMEM((steps, height, LANES), F32),
@@ -476,14 +508,15 @@
             pltpu.VMEM((slots, 2 * LANES), BF16),
             pltpu.VMEM((2 * LANES, 2 * slots), BF16),
             pltpu.VMEM((comp, GROUP * perforations), F32),
-            dma,
+            pltpu.VMEM((height, comp * perforations), BF16),
+            dma((7,)),
             dma((6, 2)),
             dma((2, 2)),
             dma((4, 2, 2)),
             dma((4, 2, 2)),
         ],
         compiler_params=pltpu.CompilerParams(
-            collective_id=0, has_side_effects=True, vmem_limit_bytes=48 * 1024 * 1024
+            collective_id=0, has_side_effects=True, vmem_limit_bytes=60 * 1024 * 1024
         ),
     )(
         flat(perm),

time: 93.6 us -> 87.2 us (0.932)
  local copies, waits for them, and re-layouts: 8.23 us -> 3.14 us
  Pallas kernels: 84.4 us -> 83.3 us
    unnamed x16 -> x2, local copies, waits for them, and re-layouts: 8.23 us -> 3.14 us
    pallas_call x1, Pallas kernels: 84.4 us -> 83.3 us  [on_device(): pl.pallas_call(functools.partial(kernel, n), out_shape=[jax.ShapeDtypeStr...]
where the time goes in v2:
time: 87.2 us; the launch traced here: 87 us
  Pallas kernels  83.3 us (96%)
  local copies, waits for them, and re-layouts  3.14 us (4%)
    pallas_call x1, Pallas kernels, on_device(): pl.pallas_call(functools.partial(kernel, n), out_shape=[jax.ShapeDtypeStr...  83.3 us
    unnamed x2, local copies, waits for them, and re-layouts  3.14 us

profile of v2, /device:TPU:1, one launch (start us, length us, event | category | flops | bytes accessed | tf_op | source)
XLA Modules:
  0.0 87.0 jit_solution(2363699274459830183)
XLA Ops:
  0.6 83.3 %shard_map.86 = (f32[128,256]{1,0:T(8,128)}, f32[128,256]{1,0:T(8,128)}) custom-call(f32[128,256]{1,0:T(8,128)} %bitcast.10, f32[128,256]{1,0:T(8,128)} %bitcast.11, f32[128,256]{1,0:T(8,128)} %bitcast.12, bf16[8192,256]{1,0:T(8,128)(2,1)} %bitcast.9, bf16[64,128]{1,0:T(8,128)(2,1)} %bitcast.15, s32[1,128]{1,0:T(1,128)} %bitcast.16, s32[1,128]{1,0:T(1,128)} %bitcast.17), custom_call_target="tpu_custom_call" | custom-call | tf_op jit(solution)/shard_map/pallas_call | solution.py:480
  83.9 1.6 %copy.11 = f32[2,64,256]{2,1,0:T(8,128)} copy(f32[2,64,256]{2,1,0:T(8,128)} %bitcast.14) | data formatting | bytes 262144
  85.5 1.6 %copy.12 = f32[2,64,256]{2,1,0:T(8,128)} copy(f32[2,64,256]{2,1,0:T(8,128)} %bitcast.13) | data formatting | bytes 262144

commit v3 on v2

--- a/solution.py
+++ b/solution.py
@@ -87,6 +87,8 @@
     halo_recv,
     hot_send,
     hot_recv,
+    rows_send,
+    rows_recv,
     data_send,
     data_recv,
     meta_send,
@@ -100,6 +102,7 @@
     load_sem,
     halo_sem,
     hot_sem,
+    rows_sem,
     data_sem,
     meta_sem,
 ):
@@ -326,6 +329,24 @@
                 dot = dot + both[:, i : i + LANES]
         return jnp.concatenate(backs, axis=0), dot
 
+    def start_rows(which, v):
+        rows_send[which] = v.astype(BF16).reshape(chips, 8, LANES)
+        rows_recv[which, 0, pl.ds(chip, 1)] = rows_send[which, pl.ds(chip, 1)]
+        to_chips(
+            lambda q: send(
+                rows_send.at[which, q],
+                rows_recv.at[which, 0, chip],
+                rows_sem.at[which, 0],
+                q * 2 + core,
+            )
+        )
+
+    def finish_rows(which):
+        copy = swap(rows_recv.at[which], rows_sem.at[which])
+        total = nn(take_ref[:, :slots], rows_recv[which, 0].reshape(slots, LANES))
+        copy.wait_recv()
+        return total + nn(take_ref[:, slots:], rows_recv[which, 1].reshape(slots, LANES))
+
     def start_exchange(which, v, sums):
         largest = jnp.maximum(jnp.max(jnp.max(jnp.abs(v), axis=0, keepdims=True), axis=1, keepdims=True), 1e-30)
         fixed = jnp.round(v * (LARGEST / largest))
@@ -348,7 +369,8 @@
         await_bytes(ref.at[0, pl.ds(0, chips - 1)], sems.at[0, 1])
         return send(ref.at[0], ref.at[1], sems.at[1], sibling)
 
-    def finish_exchange(which, weights):
+    def finish_exchange(which):
+        weights = scatter_ref
         data = data_recv.at[which]
         meta = meta_recv.at[which]
         data_swap = swap(data, data_sem.at[which])
@@ -382,8 +404,7 @@
     z0 = precondition(r0)
 
     hot_swap = swap(hot_recv, hot_sem)
-    z0_cols = columns_of(z0)
-    z0_high, z0_low = split(z0_cols)
+    z0_cols = columns_of(z0).astype(BF16)
     hot_swap.wait_recv()
     codes = jnp.concatenate([hot_recv[0, :, 0, :], hot_recv[1, :, 0, :]], axis=0).astype(BF16)
     r = iota((slots, 2 * chips), 0)
@@ -399,7 +420,7 @@
     gather_ref[...] = jnp.concatenate(
         [jnp.where(upper, 0.0, asked), jnp.where(upper, asked, 0.0)], axis=1
     ).astype(BF16)
-    start_exchange(0, nn(gather_ref[...], z0_high) + nn(gather_ref[...], z0_low), [])
+    start_rows(0, nn(gather_ref[...], z0_cols))
     halo0 = start_halo(z0, 0)
 
     r = iota((2 * chips, 2 * slots), 1)
@@ -428,37 +449,37 @@
     s0 = stencil(z0, 0, halo0)
     rz_part = fold(r0 * z0)
     zs_part = fold(z0 * s0)
-    rows, _ = finish_exchange(0, take_ref)
-    rows0 = side_by_side(rows)
-    back, yu = wells(rows0)
-    start_exchange(1, picked(give_ref[...], stacked(back)), [rz_part, zs_part + yu])
-    added, sums = finish_exchange(1, scatter_ref)
+    back, yu = wells(side_by_side(finish_rows(0)))
+    start_exchange(0, picked(give_ref[...], stacked(back)), [rz_part, zs_part + yu])
+    added, sums = finish_exchange(0)
     rz0, g00 = sums[:, 1:2], sums[:, 2:3]
     alpha0 = rz0 / g00
     w0 = jnp.concatenate([added[:LANES].T, added[LANES:].T], axis=0)
-    r1 = r0 - alpha0 * (s0 + w0)
+    q0 = s0 + w0
+    r1 = r0 - alpha0 * q0
     z1 = precondition(r1)
 
-    start_exchange(2, picked(gather_ref[...], columns_of(z1)), [fold(r1 * z1)])
+    start_rows(1, nn(gather_ref[...], columns_of(z1).astype(BF16)))
     halo1 = start_halo(z1, 1)
     s1 = stencil(z1, 1, halo1)
-    rows, sums = finish_exchange(2, take_ref)
+    fresh_part = fold(r1 * z1)
+    zq_part = fold(z1 * q0)
+    zs_part = fold(z1 * s1)
+    back, yu = wells(side_by_side(finish_rows(1)))
+    start_exchange(1, picked(give_ref[...], stacked(back)), [fresh_part, zs_part + yu, zq_part])
+    added, sums = finish_exchange(1)
     fresh = sums[:, 1:2]
     beta = fresh / rz0
-    back, yu = wells(side_by_side(rows) + beta * rows0)
-    d1 = z1 + beta * z0
-    image = s1 + beta * s0
-    start_exchange(3, picked(give_ref[...], stacked(back)), [fold(d1 * image) + yu])
-    added, sums = finish_exchange(3, scatter_ref)
-    alpha1 = fresh / sums[:, 1:2]
-    sol_ref[...] = (alpha0 * z0 + alpha1 * d1).T
+    alpha1 = fresh / (sums[:, 2:3] + 2.0 * beta * sums[:, 3:4] + beta * beta * g00)
+    sol_ref[...] = (alpha0 * z0 + alpha1 * (z1 + beta * z0)).T
     w1 = jnp.concatenate([added[:LANES].T, added[LANES:].T], axis=0)
-    res_ref[...] = (r1 - alpha1 * (image + w1)).T
+    res_ref[...] = (r1 - alpha1 * (s1 + beta * q0 + w1)).T
 
     for copy in (perm_right, perm_left, *halo0, *halo1):
         copy.wait_send()
     drain(hot_recv, hot_recv, hot_sem)
-    for i in range(4):
+    for i in range(2):
+        drain(rows_recv.at[i], rows_recv.at[i], rows_sem.at[i])
         drain(data_recv.at[i], data_recv.at[i], data_sem.at[i])
         drain(meta_recv.at[i], meta_recv.at[i], meta_sem.at[i])
 
@@ -499,10 +520,12 @@
             pltpu.VMEM((2, 2, height // 2, LANES), F32),
             pltpu.VMEM((chips, 1, LANES), F32),
             pltpu.VMEM((2, chips, 1, LANES), F32),
-            pltpu.VMEM((4, chips, 8, LANES), jnp.int16),
-            pltpu.VMEM((4, 2, chips, 8, LANES), jnp.int16),
-            pltpu.VMEM((4, 1, LANES), F32),
-            pltpu.VMEM((4, 2, chips, 1, LANES), F32),
+            pltpu.VMEM((2, chips, 8, LANES), BF16),
+            pltpu.VMEM((2, 2, chips, 8, LANES), BF16),
+            pltpu.VMEM((2, chips, 8, LANES), jnp.int16),
+            pltpu.VMEM((2, 2, chips, 8, LANES), jnp.int16),
+            pltpu.VMEM((2, 1, LANES), F32),
+            pltpu.VMEM((2, 2, chips, 1, LANES), F32),
             pltpu.VMEM((2 * comp, 2 * slots), BF16),
             pltpu.VMEM((slots, 2 * comp), BF16),
             pltpu.VMEM((slots, 2 * LANES), BF16),
@@ -512,8 +535,9 @@
             dma((7,)),
             dma((6, 2)),
             dma((2, 2)),
-            dma((4, 2, 2)),
-            dma((4, 2, 2)),
+            dma((2, 2, 2)),
+            dma((2, 2, 2)),
+            dma((2, 2, 2)),
         ],
         compiler_params=pltpu.CompilerParams(
             collective_id=0, has_side_effects=True, vmem_limit_bytes=60 * 1024 * 1024

time: 87.2 us -> 83.6 us (0.959)
  Pallas kernels: 83.3 us -> 79.6 us
    pallas_call x1, Pallas kernels: 83.3 us -> 79.6 us  [on_device(): pl.pallas_call(functools.partial(kernel, n), out_shape=[jax.ShapeDtypeStr...]
where the time goes in v3:
time: 83.6 us; the launch traced here: 83.4 us
  Pallas kernels  79.6 us (95%)
  local copies, waits for them, and re-layouts  3.14 us (4%)
    pallas_call x1, Pallas kernels, on_device(): pl.pallas_call(functools.partial(kernel, n), out_shape=[jax.ShapeDtypeStr...  79.6 us
    unnamed x2, local copies, waits for them, and re-layouts  3.14 us

profile of v3, /device:TPU:1, one launch (start us, length us, event | category | flops | bytes accessed | tf_op | source)
XLA Modules:
  0.0 83.4 jit_solution(5814211845244958083)
XLA Ops:
  0.6 79.6 %shard_map.86 = (f32[128,256]{1,0:T(8,128)}, f32[128,256]{1,0:T(8,128)}) custom-call(f32[128,256]{1,0:T(8,128)} %bitcast.10, f32[128,256]{1,0:T(8,128)} %bitcast.11, f32[128,256]{1,0:T(8,128)} %bitcast.12, bf16[8192,256]{1,0:T(8,128)(2,1)} %bitcast.9, bf16[64,128]{1,0:T(8,128)(2,1)} %bitcast.15, s32[1,128]{1,0:T(1,128)} %bitcast.16, s32[1,128]{1,0:T(1,128)} %bitcast.17), custom_call_target="tpu_custom_call" | custom-call | tf_op jit(solution)/shard_map/pallas_call | solution.py:501
  80.3 1.6 %copy.11 = f32[2,64,256]{2,1,0:T(8,128)} copy(f32[2,64,256]{2,1,0:T(8,128)} %bitcast.14) | data formatting | bytes 262144
  81.8 1.6 %copy.12 = f32[2,64,256]{2,1,0:T(8,128)} copy(f32[2,64,256]{2,1,0:T(8,128)} %bitcast.13) | data formatting | bytes 262144

commit v4 on v3

--- a/solution.py
+++ b/solution.py
@@ -69,8 +69,7 @@
     gains_hbm,
     target_hbm,
     column_hbm,
-    sol_ref,
-    res_ref,
+    out_ref,
     perm_ref,
     storage_ref,
     right_ref,
@@ -122,6 +121,46 @@
     slots = chips * 8
     steps = alpha_ref.shape[0]
 
+    def greet(device):
+        pl.semaphore_signal(
+            pltpu.get_barrier_semaphore(),
+            inc=1,
+            device_id={"cells": device},
+            device_id_type=pl.DeviceIdType.MESH,
+        )
+
+    def send(src, dst, sems, device):
+        copy = pltpu.make_async_remote_copy(
+            src_ref=src,
+            dst_ref=dst,
+            send_sem=sems.at[0],
+            recv_sem=sems.at[1],
+            device_id={"cells": device},
+            device_id_type=pl.DeviceIdType.MESH,
+        )
+        copy.start()
+        return copy
+
+    def await_bytes(ref, sem):
+        pltpu.make_async_copy(ref, ref, sem).wait()
+
+    def to_chips(act):
+        def plane(j, carry):
+            away = along_z // 2 + (j % 2) * (j // 2) - (1 - j % 2) * (j // 2)
+            z = lax.rem(z_here + away, along_z)
+            for across in (2, 1, 3, 0):
+                act(z * ALONG_Y + lax.rem(y_here + across, ALONG_Y))
+            return carry
+
+        lax.fori_loop(1, along_z, plane, 0)
+        for across in (2, 1, 3):
+            act(z_here * ALONG_Y + lax.rem(y_here + across, ALONG_Y))
+
+    to_chips(lambda q: greet(q * 2 + core))
+    greet(left)
+    greet(right)
+    greet(sibling)
+
     loads = [
         pltpu.make_async_copy(src, dst, load_sem.at[i])
         for i, (src, dst) in enumerate(
@@ -138,46 +177,6 @@
     ]
     for load in loads:
         load.start()
-
-    def greet(device):
-        pl.semaphore_signal(
-            pltpu.get_barrier_semaphore(),
-            inc=1,
-            device_id={"cells": device},
-            device_id_type=pl.DeviceIdType.MESH,
-        )
-
-    def send(src, dst, sems, device):
-        copy = pltpu.make_async_remote_copy(
-            src_ref=src,
-            dst_ref=dst,
-            send_sem=sems.at[0],
-            recv_sem=sems.at[1],
-            device_id={"cells": device},
-            device_id_type=pl.DeviceIdType.MESH,
-        )
-        copy.start()
-        return copy
-
-    def await_bytes(ref, sem):
-        pltpu.make_async_copy(ref, ref, sem).wait()
-
-    def to_chips(act):
-        def plane(j, carry):
-            away = along_z // 2 + (j % 2) * (j // 2) - (1 - j % 2) * (j // 2)
-            z = lax.rem(z_here + away, along_z)
-            for across in (2, 1, 3, 0):
-                act(z * ALONG_Y + lax.rem(y_here + across, ALONG_Y))
-            return carry
-
-        lax.fori_loop(1, along_z, plane, 0)
-        for across in (2, 1, 3):
-            act(z_here * ALONG_Y + lax.rem(y_here + across, ALONG_Y))
-
-    to_chips(lambda q: greet(q * 2 + core))
-    greet(left)
-    greet(right)
-    greet(sibling)
 
     for load in loads[:6]:
         load.wait()
@@ -471,9 +470,9 @@
     fresh = sums[:, 1:2]
     beta = fresh / rz0
     alpha1 = fresh / (sums[:, 2:3] + 2.0 * beta * sums[:, 3:4] + beta * beta * g00)
-    sol_ref[...] = (alpha0 * z0 + alpha1 * (z1 + beta * z0)).T
+    out_ref[0] = (alpha0 * z0 + alpha1 * (z1 + beta * z0)).T
     w1 = jnp.concatenate([added[:LANES].T, added[LANES:].T], axis=0)
-    res_ref[...] = (r1 - alpha1 * (s1 + beta * q0 + w1)).T
+    out_ref[1] = (r1 - alpha1 * (s1 + beta * q0 + w1)).T
 
     for copy in (perm_right, perm_left, *halo0, *halo1):
         copy.wait_send()
@@ -498,11 +497,11 @@
 
     vmem = pl.BlockSpec(memory_space=pltpu.VMEM)
     dma = pltpu.SemaphoreType.DMA
-    sol, res = pl.pallas_call(
+    out = pl.pallas_call(
         functools.partial(kernel, n),
-        out_shape=[jax.ShapeDtypeStruct((columns, height), F32)] * 2,
+        out_shape=jax.ShapeDtypeStruct((2, columns, height), F32),
         in_specs=[pl.BlockSpec(memory_space=pl.ANY)] * 7,
-        out_specs=[vmem] * 2,
+        out_specs=vmem,
         scratch_shapes=[
             pltpu.VMEM((columns, height), F32),
             pltpu.VMEM((columns, height), F32),
@@ -551,7 +550,7 @@
         well_target.reshape(1, comp),
         well_column.reshape(1, comp),
     )
-    return sol.reshape(shape), res.reshape(shape)
+    return out[0].reshape(shape), out[1].reshape(shape)
 
 
 def solution(mesh):

time: 83.6 us -> 82.3 us (0.984)
  local copies, waits for them, and re-layouts: 3.14 us -> 1.69 us
    unnamed x2 -> x0, local copies, waits for them, and re-layouts: 3.14 us -> none
    slice x0 -> x1, local copies, waits for them, and re-layouts: none -> 1.69 us  [on_device(): return (out[0].reshape(shape), out[1].reshape(shape))]
where the time goes in v4:
time: 82.3 us; the launch traced here: 82.1 us
  Pallas kernels  79.8 us (97%)
  local copies, waits for them, and re-layouts  1.69 us (2%)
    pallas_call x1, Pallas kernels, on_device(): pl.pallas_call(functools.partial(kernel, n), out_shape=jax.ShapeDtypeStru...  79.8 us
    slice x1, local copies, waits for them, and re-layouts, on_device(): return (out[0].reshape(shape), out[1].reshape(shape))  1.69 us

profile of v4, /device:TPU:1, one launch (start us, length us, event | category | flops | bytes accessed | tf_op | source)
XLA Modules:
  0.0 82.1 jit_solution(14011178100924925718)
XLA Ops:
  0.6 79.8 %shard_map.86 = f32[2,128,256]{2,1,0:T(8,128)} custom-call(f32[128,256]{1,0:T(8,128)} %bitcast.10, f32[128,256]{1,0:T(8,128)} %bitcast.11, f32[128,256]{1,0:T(8,128)} %bitcast.12, bf16[8192,256]{1,0:T(8,128)(2,1)} %bitcast.9, bf16[64,128]{1,0:T(8,128)(2,1)} %bitcast.15, s32[1,128]{1,0:T(1,128)} %bitcast.16, s32[1,128]{1,0:T(1,128)} %bitcast.17), custom_call_target="tpu_custom_call" | custom-call | tf_op jit(solution)/shard_map/pallas_call | solution.py:500
  80.4 1.7 %fusion = (f32[1,128,256]{2,1,0:T(8,128)}, f32[1,128,256]{2,1,0:T(8,128)}) fusion(f32[2,128,256]{2,1,0:T(8,128)} %shard_map.86), kind=kLoop, calls=%fused_computation | loop fusion | bytes 524288 | tf_op jit(solution)/shard_map/slice | solution.py:553
